TPU v7x, 32 devices: a whole 2x2x4 slice. The times are simulated.
32 devices in a mesh: groups: 2 (over y), tp: 4 (over z), pp: 2 (over x), dp: 2 (over core).
Axes of the slice: x: 2, y: 2, z: 4, core: 2. Of those that a mesh axis runs over, the one named last changes fastest.
Arguments:
- hidden: bfloat16 [4, 4, 64, 5120], P(('groups', 'pp'), None, 'dp', 'tp'), parts along dimension 0, may hold values from -6 to 6
- w_kv: bfloat16 [4, 5120, 2048], P(('groups', 'pp'), 'tp'), parts along dimension 0, may hold values from -0.078125 to 0.078125
- queries: bfloat16 [4, 4, 64, 4096], P(('groups', 'pp'), None, 'dp', 'tp'), parts along dimension 0, may hold values from -8 to 8
- cache: bfloat16 [4, 64, 16, 128, 256], P(('groups', 'pp'), 'dp', 'tp'), parts along dimension 0, may hold values from -4 to 4
- cache_lengths: int32 [128], P(('groups', 'dp')), parts along dimension 0, may hold values from 2 to 256
- updated: int32 [4, 5120], P(('groups', 'pp'), 'tp'), parts along dimension 0, may hold values from 0 to 1, as said below
- delta_values: bfloat16 [32, 8, 8, 128], P(('groups', 'tp', 'pp', 'dp')), parts along dimension 0, may hold values from -4 to 4
- delta_scales: bfloat16 [32, 8, 8], P(('groups', 'tp', 'pp', 'dp')), parts along dimension 0, may hold values from 0.0039978027 to 0.039794922
- delta_targets: int32 [32, 8, 8], P(('groups', 'tp', 'pp', 'dp')), parts along dimension 0, may hold values from 0 to 20479
- send_counts: int32 [32, 8], P(('groups', 'tp', 'pp', 'dp')), parts along dimension 0, may hold values from 0 to 8, as said below
Outputs:
- new_entries: bfloat16 [4, 4, 64, 2048], P(('groups', 'pp'), None, 'dp', 'tp'), parts along dimension 0
- attention_out: bfloat16 [4, 4, 64, 4096], P(('groups', 'pp'), None, 'dp', 'tp'), parts along dimension 0
There are 2 independent parts, one for each index of `groups`. A program takes and returns all parts, laid end to end along the dimension named above; each array names one. Nothing has to cross between parts.
Inputs may be any that keep to these rules, and one draw needn't show every extreme that they name: `send_counts`: at most 8; every sender fills all 8 slots of some owner, and one owner receives 8 live blocks from every sender. `updated`: rows of all but half of the 2 layers, rounded down, are 0.
All inputs are finite; a program needn't handle non-finite values.
Results may differ from a plain program's by a relative error of at most 0.01.
Values may be sent and summed in bfloat16 or wider, within the bound.
A program may use at most 128 MiB of HBM per device.

v0:
```python
import math

import jax
import jax.numpy as jnp
from jax import lax
from jax.sharding import PartitionSpec as P

ROPE_BASE = 1000000.0
NEG_FILL = -1e30


def from_partner(x, axis, apart):
    return lax.ppermute(x, axis, [(i, i ^ 1 << apart) for i in range(lax.axis_size(axis))])


def rotate(vectors, positions):
    half_size = vectors.shape[-1] // 2
    index_f = jnp.arange(half_size).astype(jnp.float32)
    inverse = jnp.exp(index_f * (-2.0 / vectors.shape[-1]) * math.log(ROPE_BASE))
    angles = positions[..., None] * inverse
    cosine_table = jnp.cos(angles)
    sine_table = jnp.sin(angles)
    first_half = vectors[..., :half_size]
    second_half = vectors[..., half_size:]
    return jnp.concatenate(
        [
            first_half * cosine_table - second_half * sine_table,
            second_half * cosine_table + first_half * sine_table,
        ],
        -1,
    )


def softmax_block(scores, valid, value_rows, value_form):
    scores = jnp.where(valid, scores, NEG_FILL)
    row_max = jnp.max(scores, -1)
    weights = jnp.where(valid, jnp.exp(scores - row_max[..., None]), jnp.float32(0.0))
    weighted = jnp.einsum(
        value_form, weights, value_rows.astype(jnp.float32), precision=lax.Precision.HIGHEST
    )
    return (row_max, jnp.sum(weights, -1), weighted)


def cache_block(query_rows, cache_rows, cache_lengths, score_scale):
    head_dim = cache_rows.shape[-1] // 2
    slot_index = jnp.arange(cache_rows.shape[2], dtype=jnp.int32)
    valid = (slot_index[None, :] < cache_lengths[:, None])[None, :, None, None, :]
    scores = (
        jnp.einsum(
            "trgbd,rgpd->trgbp",
            query_rows,
            cache_rows[..., :head_dim],
            preferred_element_type=jnp.float32,
        )
        * score_scale
    )
    return softmax_block(scores, valid, cache_rows[..., head_dim:], "trgbp,rgpd->trgbd")


def shards(
    hidden,
    w_kv,
    queries,
    cache,
    cache_lengths,
    updated,
    delta_values,
    delta_scales,
    delta_targets,
    send_counts,
):
    slot_count = delta_values.shape[2]
    block_width = delta_values.shape[3]
    shard_rows = w_kv.shape[1]
    kv_width = w_kv.shape[2]
    step_count = hidden.shape[1]
    rows_dev = hidden.shape[2]
    head_dim = cache.shape[4] // 2
    local_heads = cache.shape[2]
    live_slots = jnp.arange(slot_count, dtype=jnp.int32)[None, :] < send_counts[0][:, None]
    sent_scales = jnp.where(live_slots, delta_scales[0], jnp.zeros((), jnp.bfloat16))
    got_values, got_scales, got_targets = (
        lax.all_to_all(delta_values[0], ("tp", "pp"), split_axis=0, concat_axis=0, tiled=True),
        lax.all_to_all(sent_scales, ("tp", "pp"), split_axis=0, concat_axis=0, tiled=True),
        lax.all_to_all(delta_targets[0], ("tp", "pp"), split_axis=0, concat_axis=0, tiled=True),
    )
    all_values, all_scales, all_targets = (
        lax.all_gather(got_values[None], "dp", axis=0, tiled=True),
        lax.all_gather(got_scales[None], "dp", axis=0, tiled=True),
        lax.all_gather(got_targets[None], "dp", axis=0, tiled=True),
    )
    contribution = all_values.astype(jnp.float32) * all_scales.astype(jnp.float32)[..., None]
    dense_delta = jnp.zeros((shard_rows * kv_width // block_width, block_width), jnp.float32)
    dense_delta = dense_delta.at[all_targets.reshape(-1)].add(contribution.reshape(-1, block_width))
    merged = (w_kv[0].astype(jnp.float32) + dense_delta.reshape(shard_rows, kv_width)).astype(
        jnp.bfloat16
    )
    weight = jnp.where(updated[0][:, None] == 1, merged, w_kv[0])
    flat_rows = hidden[0].reshape(step_count * rows_dev, shard_rows)
    tp_count = lax.axis_size("tp")
    tp_index = lax.axis_index("tp")
    half_count = tp_count // 2
    upper_half = tp_index // half_count
    head_group = tp_index % half_count
    partner_bit = tp_count.bit_length() - 2
    piece_width = kv_width // tp_count
    step_index = jnp.arange(step_count, dtype=jnp.int32)
    positions = (cache_lengths[None, :] + step_index[:, None]).astype(jnp.float32)
    summed = lax.psum(
        jnp.dot(flat_rows, weight, preferred_element_type=jnp.float32).astype(jnp.bfloat16), "tp"
    ).astype(jnp.float32)
    summed = summed.reshape(step_count, rows_dev, 2, kv_width // (2 * head_dim), head_dim)
    keys_all = rotate(summed[:, :, 0], positions[:, :, None]).astype(jnp.bfloat16)
    values_all = summed[:, :, 1].astype(jnp.bfloat16)
    entries = jnp.stack([keys_all, values_all], 2).reshape(step_count, rows_dev, kv_width)
    own_entries = lax.dynamic_slice_in_dim(entries, tp_index * piece_width, piece_width, 2)
    new_keys = lax.dynamic_slice_in_dim(keys_all, head_group * local_heads, local_heads, 2)
    new_values = lax.dynamic_slice_in_dim(values_all, head_group * local_heads, local_heads, 2)
    score_scale = 1.0 / math.sqrt(head_dim)
    query_rows = queries[0].reshape(step_count, rows_dev, local_heads, 2, head_dim)
    own_cache = cache[0]
    partner_cache = from_partner(own_cache, "tp", partner_bit)
    lower_cache = jnp.where(upper_half == 0, own_cache, partner_cache)
    higher_cache = jnp.where(upper_half == 0, partner_cache, own_cache)
    whole_cache = jnp.concatenate([lower_cache, higher_cache], 2)
    partial_blocks = [cache_block(query_rows, whole_cache, cache_lengths, score_scale)]
    fresh_scores = (
        jnp.einsum("trgbd,urgd->trgbu", query_rows, new_keys, preferred_element_type=jnp.float32)
        * score_scale
    )
    fresh_valid = (step_index[None, :] <= step_index[:, None])[:, None, None, None, :]
    partial_blocks.append(softmax_block(fresh_scores, fresh_valid, new_values, "trgbu,urgd->trgbd"))
    block_max = jnp.stack([entry[0] for entry in partial_blocks], 0)
    overall_max = jnp.max(block_max, 0)
    row_total = jnp.zeros_like(overall_max)
    weighted = jnp.zeros(partial_blocks[0][2].shape, jnp.float32)
    for entry in partial_blocks:
        rescale = jnp.exp(entry[0] - overall_max)
        row_total = row_total + entry[1] * rescale
        weighted = weighted + entry[2] * rescale[..., None]
    attention_rows = (weighted / row_total[..., None]).astype(jnp.bfloat16)
    attention_rows = attention_rows.reshape(step_count, rows_dev, local_heads * 2 * head_dim)
    return (own_entries[None], attention_rows[None])


def solution(mesh):
    placed = (
        P(("groups", "pp"), None, "dp", "tp"),
        P(("groups", "pp"), "tp", None),
        P(("groups", "pp"), None, "dp", "tp"),
        P(("groups", "pp"), "dp", "tp", None, None),
        P(("groups", "dp")),
        P(("groups", "pp"), "tp"),
        P(("groups", "tp", "pp", "dp"), None, None, None),
        P(("groups", "tp", "pp", "dp"), None, None),
        P(("groups", "tp", "pp", "dp"), None, None),
        P(("groups", "tp", "pp", "dp"), None),
    )
    return jax.shard_map(
        shards,
        mesh=mesh,
        in_specs=placed,
        out_specs=(P(("groups", "pp"), None, "dp", "tp"), P(("groups", "pp"), None, "dp", "tp")),
        check_vma=False,
    )
```

profile of v0, /device:TPU:0, one launch (start us, length us, event | category | flops | bytes accessed | tf_op | source)
XLA Modules:
  0.0 502.9 jit_solution(10467981817925615663)
XLA Ops:
  7.2 4.1 collective-permute-start
  12.6 3.8 all-to-all-start.2
  16.4 1.1 reshape_squeeze.7
  19.0 353.7 %all-to-all-done.2 = bf16[8,1,8]{2,1,0:T(2,128)(2,1)S(1)} async-done(((bf16[8,1,8]{2,1,0:T(2,128)(2,1)}), bf16[8,1,8]{2,1,0:T(2,128)(2,1)S(1)}, u32[]{:S(2)}, u32[]{:S(2)}) %all-to-all-start.2) | async-done | bytes 160 | tf_op jit(solution)/shard_map/all_to_all | solution.py:84
  372.7 4.9 all-to-all-start
  377.6 1.8 all-gather.2
  379.6 4.4 all-to-all-done
  384.0 3.3 all-to-all-start.1
  387.4 1.8 all-gather
  390.5 3.4 all-to-all-done.1
  393.9 1.8 all-gather.1
  395.8 5.6 %scatter_custom_fusion = f32[20480,128]{1,0:T(8,128)} fusion(s32[128]{0:T(128)S(1)} %fusion.67, f32[128,128]{1,0:T(8,128)S(1)} %bitcast.122, f32[]{:T(128)} %constant.20.clone.1), kind=kCustom, calls=%fused_computation.15 | custom fusion | flops 16384 | bytes 10485764 | tf_op jit(solution)/shard_map/scatter-add | solution.py:94
  401.4 11.4 %reshape.261 = f32[1,1280,2048]{2,1,0:T(8,128)} reshape(f32[20480,128]{1,0:T(8,128)} %scatter_custom_fusion) | data formatting | bytes 20971520 | tf_op jit(solution)/shard_map/reshape | solution.py:95
  412.8 10.1 %fusion.17 = bf16[128,2048]{0,1:T(8,128)(2,1)S(1)} fusion(bf16[128,1280]{1,0:T(8,128)(2,1)S(1)} %bitcast.108, bf16[1,1280,2048]{2,1,0:T(8,128)(2,1)} %param.11, f32[1,1280,2048]{2,1,0:T(8,128)} %reshape.261, pred[1280]{0:T(1024)(128)(4,1)S(1)} %compare_reduce_fusion), kind=kOutput, calls=%fused_computation.19 | convolution fusion | flops 681836544 | bytes 16581888 | tf_op jit(solution)/shard_map/dot_general | solution.py:110
  423.3 1.5 copy.73
  425.5 35.7 %all-reduce.2.cloned.1.call-done = bf16[4,32,2,8,128]{4,0,3,1,2:T(4,128)(2,1)} async-done(((bf16[4,32,2,8,128]{4,0,3,1,2:T(4,128)(2,1)}), bf16[4,32,2,8,128]{4,0,3,1,2:T(4,128)(2,1)}) %all-reduce.2.cloned.1.call-update) | async-done | bytes 524304 | tf_op jit(solution)/shard_map/psum | solution.py:109
  461.2 1.0 slice.66
  462.2 1.2 reshape.263
  464.7 2.5 fusion.75
  468.7 11.3 %broadcast_select_fusion.1 = (bf16[32,4,128,256]{3,2,1,0:T(8,128)(2,1)}, bf16[32,4,128,256]{3,2,1,0:T(8,128)(2,1)}) fusion(bf16[32,4,128,256]{3,2,1,0:T(8,128)(2,1)} %collective-permute-done, pred[]{:T(512)S(6)} %eq.23, bf16[1,32,4,128,256]{4,3,2,1,0:T(8,128)(2,1)} %param.13), kind=kLoop, calls=%fused_computation.11 | loop fusion | flops 8388608 | bytes 33554432 | tf_op jit(solution)/shard_map/jit(_where)/select_n | solution.py:123
  480.0 5.9 %fusion.76 = (f32[4,32,4,2]{0,3,2,1:T(2,128)S(1)}, f32[4,32,4,2,256]{4,0,3,2,1:T(4,128)S(1)}) fusion(bf16[4,32,4,2,128]{4,3,2,1,0:T(2,128)(2,1)S(1)} %reshape_squeeze.7, bf16[32,4,128,256]{3,2,1,0:T(8,128)(2,1)} %get-tuple-element.6, bf16[32,4,128,256]{3,2,1,0:T(8,128)(2,1)} %get-tuple-element.5, pred[32,256]{1,0:T(8,128)(4,1)S(1)} %iota_compare_fusion), kind=kOutput, calls=%fused_computation.82 | convolution fusion | flops 84671488 | bytes 18100224 | tf_op jit(solution)/shard_map/trgbd,rgpd->trgbp/dot_general | solution.py:49
  487.2 1.3 fusion.28
  488.9 6.1 %fusion.44 = bf16[4,32,4,2,128]{4,0,3,2,1:T(4,128)(2,1)S(1)} fusion(f32[4,32,4,2,128]{4,0,3,2,1:T(4,128)S(1)} %fusion.28, bf16[32,4,128,256]{3,2,1,0:T(8,128)(2,1)} %get-tuple-element.5, bf16[32,4,128,256]{3,2,1,0:T(8,128)(2,1)} %get-tuple-element.6, f32[4,32,4,2,256]{4,0,3,2,1:T(4,128)S(1)} %get-tuple-element.14, ...), kind=kOutput, calls=%fused_computation.33 | convolution fusion | flops 420478976 | bytes 18632704 | tf_op jit(solution)/shard_map/trgbp,rgpd->trgbd/dot_general | solution.py:38
  495.2 0.9 broadcast_in_dim_reshape.3
  (44 shorter events, 9.9 us)
Async XLA Ops:
  7.2 405.7 %copy-start = (bf16[1,4,32,1280]{3,2,1,0:T(8,128)(2,1)S(1)}, bf16[1,4,32,1280]{3,2,1,0:T(8,128)(2,1)}, u32[]{:S(2)}) copy-start(bf16[1,4,32,1280]{3,2,1,0:T(8,128)(2,1)} %param.10) | copy-start | bytes 983044
  7.2 461.5 %collective-permute-start = (bf16[32,4,128,256]{3,2,1,0:T(8,128)(2,1)}, bf16[32,4,128,256]{3,2,1,0:T(8,128)(2,1)}, u32[]{:S(2)}, u32[]{:S(2)}) collective-permute-start(bf16[32,4,128,256]{3,2,1,0:T(8,128)(2,1)} %bitcast.109), channel_id=1, source_target_pairs={{0,8},{4,12},{8,0},{12,4},{1,9},{5,13},{9,1},{13,5},{2,10},{6,14},... | collective-permute-start | bytes 25165832 | tf_op jit(solution)/shard_map/ppermute | solution.py:13
  12.6 360.1 %all-to-all-start.2 = ((bf16[8,1,8]{2,1,0:T(2,128)(2,1)}), bf16[8,1,8]{2,1,0:T(2,128)(2,1)S(1)}, u32[]{:S(2)}, u32[]{:S(2)}) async-start(bf16[8,1,8]{2,1,0:T(2,128)(2,1)} %copy.68), calls=%async_computation.2 | async-start | bytes 8192 | tf_op jit(solution)/shard_map/all_to_all | solution.py:84
  372.7 11.3 %all-to-all-start = ((s32[8,1,8]{2,1,0:T(1,128)}), s32[8,1,8]{2,1,0:T(1,128)S(1)}, u32[]{:S(2)}, u32[]{:S(2)}) async-start(s32[8,1,8]{2,1,0:T(1,128)} %bitcast.125), calls=%async_computation | async-start | bytes 8192 | tf_op jit(solution)/shard_map/all_to_all | solution.py:85
  384.0 9.9 %all-to-all-start.1 = ((bf16[8,8,128]{2,1,0:T(8,128)(2,1)}), bf16[8,8,128]{2,1,0:T(8,128)(2,1)S(1)}, u32[]{:S(2)}, u32[]{:S(2)}) async-start(bf16[8,8,128]{2,1,0:T(8,128)(2,1)} %bitcast.124), calls=%async_computation.1 | async-start | bytes 32768 | tf_op jit(solution)/shard_map/all_to_all | solution.py:83
  387.4 73.8 %all-reduce.2.cloned.1.call-start = ((), (), s32[]{:S(2)}) async-start(), calls=%async_computation.3 | async-start | bytes 1048576 | tf_op jit(solution)/shard_map/psum | solution.py:109
  412.8 12.0 %copy-start.2 = (s32[32]{0:T(128)S(1)}, s32[32]{0:T(128)}, u32[]{:S(2)}) copy-start(s32[32]{0:T(128)} %param.14) | copy-start | bytes 388
  488.9 7.2 %copy-start.1 = (bf16[1,4,32,1280]{3,2,1,0:T(8,128)(2,1)S(1)}, bf16[1,4,32,1280]{3,2,1,0:T(8,128)(2,1)}, u32[]{:S(2)}) copy-start(bf16[1,4,32,1280]{3,2,1,0:T(8,128)(2,1)} %param.10) | copy-start | bytes 983044
Sparse Core Ops, SparseCore 0:
  424.9 36.2 all-reduce.1
where the time goes:
time: 504 us; the launch traced here: 503 us
  waiting for transfers between devices  397 us (79%)
  matrix products  25.9 us (5%)
  other arithmetic  24.1 us (5%)
  local copies, waits for them, and re-layouts  19.9 us (4%)
  starting transfers between devices  16.2 us (3%)
  between operations  14.3 us (3%)
  blocking collectives  5.39 us (1%)
    all_to_all x1, waiting for transfers between devices, shards(): lax.all_to_all(sent_scales, ('tp', 'pp'), split_axis=0, concat_axis=0, ti...  354 us
    psum x1, waiting for transfers between devices, shards(): lax.psum(jnp.dot(flat_rows, weight, preferred_element_type=jnp.float32).a...  35.7 us
    reshape x1, local copies, waits for them, and re-layouts, shards(): dense_delta.reshape(shard_rows, kv_width)  11.4 us
    select_n x1, other arithmetic, shards(): lower_cache = jnp.where(upper_half == 0, own_cache, partner_cache)  11.3 us
    dot_general x1, matrix products, shards(): jnp.dot(flat_rows, weight, preferred_element_type=jnp.float32)  10.1 us
  transfers between devices with their start and end apart: 5, of which 4 were waited for; matrix products, arithmetic and copies ran while one was open for 8% of the time, Pallas kernels for 0%

commit v1 on v0

v1 whole, which is shorter than its diff:
```python
import functools
import math

import jax
import jax.numpy as jnp
from jax import lax
from jax.experimental import pallas as pl
from jax.experimental.pallas import tpu as pltpu
from jax.sharding import PartitionSpec as P

ROPE_BASE = 1000000.0
NEG_FILL = -1e30
MESH = pl.DeviceIdType.MESH
NT = (((1,), (1,)), ((), ()))
PAIRS = 8


def kernel(
    dims,
    lens_ref,
    hidden_ref,
    w_hbm,
    query_ref,
    cache_hbm,
    updated_ref,
    packed_ref,
    cos_ref,
    sin_ref,
    entries_ref,
    out_ref,
    w_buf,
    cache_buf,
    delta_buf,
    product,
    send_buf,
    sum_buf,
    piece_buf,
    other_piece,
    other_query,
    back_buf,
    back_stats,
    got_buf,
    got_stats,
    own_out,
    own_max,
    own_total,
    local_sem,
    cache_sem,
    delta_send,
    delta_recv,
    query_send,
    query_recv,
    sum_send,
    sum_recv,
    back_send,
    back_recv,
    tail_send,
    tail_recv,
):
    n_tp, n_pp, n_dp, heads, rows_dev, steps = dims
    n_all = n_tp * n_pp * n_dp
    head_dim = query_ref.shape[1]
    half_positions = cache_buf.shape[2]
    tokens, width = product.shape
    piece = width // n_tp
    group_rows = rows_dev * steps * 2
    blocks = group_rows // (16 * PAIRS)
    block_rows = 16 * PAIRS
    slot_rows = 16
    tp = lax.axis_index("tp")
    me = (tp * n_pp + lax.axis_index("pp")) * n_dp + lax.axis_index("dp")
    upper = tp // (n_tp // 2)
    partner = {"tp": lax.rem(tp + n_tp // 2, n_tp)}
    scale = 1.0 / math.sqrt(head_dim)

    w_copy = pltpu.make_async_copy(w_hbm, w_buf, local_sem.at[0])
    w_copy.start()

    def cache_copy(g):
        return pltpu.make_async_copy(cache_hbm.at[:, g], cache_buf.at[g], cache_sem.at[g])

    for g in range(heads):
        cache_copy(g).start()

    def place(index):
        return {
            "tp": index // (n_pp * n_dp),
            "pp": lax.rem(index // n_dp, n_pp),
            "dp": lax.rem(index, n_dp),
        }

    barrier = pltpu.get_barrier_semaphore()

    def greet(k, carry):
        pl.semaphore_signal(
            barrier, inc=1, device_id=place(lax.rem(me + k, n_all)), device_id_type=MESH
        )
        return carry

    lax.fori_loop(1, n_all, greet, 0)
    pl.semaphore_wait(barrier, n_all - 1)

    def owner_rows(index):
        return pl.ds(pl.multiple_of((index // n_dp) * slot_rows, slot_rows), slot_rows)

    my_rows = pl.ds(pl.multiple_of(me * slot_rows, slot_rows), slot_rows)

    def delta_copy(k):
        target = lax.rem(me + k, n_all)
        return pltpu.make_async_remote_copy(
            src_ref=packed_ref.at[owner_rows(target)],
            dst_ref=delta_buf.at[my_rows],
            send_sem=delta_send.at[k],
            recv_sem=delta_recv.at[k],
            device_id=place(target),
            device_id_type=MESH,
        )

    def start_delta(k, carry):
        delta_copy(k).start()
        return carry

    lax.fori_loop(1, n_all, start_delta, 0)
    own_delta = pltpu.make_async_copy(
        packed_ref.at[owner_rows(me)], delta_buf.at[my_rows], local_sem.at[1]
    )
    own_delta.start()

    def group_slice(g):
        return pl.ds(pl.multiple_of(g * group_rows, group_rows), group_rows)

    def query_copy(g):
        return pltpu.make_async_remote_copy(
            src_ref=query_ref.at[group_slice(g)],
            dst_ref=other_query.at[group_slice(g)],
            send_sem=query_send.at[g],
            recv_sem=query_recv.at[g],
            device_id=partner,
            device_id_type=MESH,
        )

    def back_copy(g):
        return pltpu.make_async_remote_copy(
            src_ref=back_buf.at[group_slice(g)],
            dst_ref=got_buf.at[group_slice(g)],
            send_sem=back_send.at[g],
            recv_sem=back_recv.at[g],
            device_id=partner,
            device_id_type=MESH,
        )

    for g in range(heads):
        query_copy(g).start()

    hidden = hidden_ref[...]
    w_copy.wait()
    tile = 256
    for c in range(width // tile):
        cols = slice(c * tile, (c + 1) * tile)
        product[:, cols] = jnp.dot(hidden, w_buf[:, cols], preferred_element_type=jnp.float32)

    def wait_delta(k, carry):
        delta_copy(k).wait()
        return carry

    lax.fori_loop(1, n_all, wait_delta, 0)
    own_delta.wait()
    shard_rows = hidden.shape[1]
    row_index = lax.broadcasted_iota(jnp.int32, (128, shard_rows), 1).astype(jnp.float32)
    taken = jnp.broadcast_to(updated_ref[...], (128, shard_rows)) == 1

    def add_deltas(chunk, carry):
        got = delta_buf[pl.ds(pl.multiple_of(chunk * 256, 256), 256), :].astype(jnp.float32)
        got = got.reshape(16, 16, 128)
        values = got[:, :8].reshape(128, 128)
        meta = got[:, 8:].reshape(128, 128)
        row = meta[:, 1:2] * 16.0 + meta[:, 2:3]
        place_row = jnp.where((row_index == row) & taken, meta[:, 0:1], 0.0).astype(jnp.bfloat16)
        picked = lax.dot_general(hidden, place_row, NT, preferred_element_type=jnp.float32)
        high = picked.astype(jnp.bfloat16)
        low = (picked - high.astype(jnp.float32)).astype(jnp.bfloat16)
        for c in range(width // tile):
            cols = slice(c * tile, (c + 1) * tile)
            spread = jnp.concatenate(
                [
                    jnp.where(meta[:, 3:4] == float(j), values, 0.0)
                    for j in range(c * tile // 128, (c + 1) * tile // 128)
                ],
                1,
            ).astype(jnp.bfloat16)
            product[:, cols] += jnp.dot(
                high, spread, preferred_element_type=jnp.float32
            ) + jnp.dot(low, spread, preferred_element_type=jnp.float32)
        return carry

    lax.fori_loop(0, n_all // 16, add_deltas, 0)
    for j in range(n_tp):
        send_buf[j] = product[:, j * piece : (j + 1) * piece].astype(jnp.bfloat16)

    def sum_copy(k):
        target = lax.rem(tp + k, n_tp)
        return pltpu.make_async_remote_copy(
            src_ref=send_buf.at[target],
            dst_ref=sum_buf.at[k],
            send_sem=sum_send.at[k],
            recv_sem=sum_recv.at[k],
            device_id={"tp": target},
            device_id_type=MESH,
        )

    for k in range(1, n_tp):
        sum_copy(k).start()

    row16 = lax.broadcasted_iota(jnp.int32, (16, 256), 0)
    col16 = lax.broadcasted_iota(jnp.int32, (16, 256), 1)
    same = (row16 // 8) == (col16 // 128)
    position = lax.rem(col16, 128) + upper * half_positions
    eye = lax.broadcasted_iota(jnp.int32, (128, 128), 0) == lax.broadcasted_iota(
        jnp.int32, (128, 128), 1
    )

    def attend(source, g, block):
        base = block * 2 * PAIRS
        scores, valids = [], []
        start = pl.multiple_of(g * group_rows + block * block_rows, block_rows)
        for i in range(PAIRS):
            r = base + 2 * i
            keys = jnp.concatenate(
                [cache_buf[g, r, :, :head_dim], cache_buf[g, r + 1, :, :head_dim]], 0
            )
            q16 = source[pl.ds(start + 16 * i, 16), :]
            scores.append(lax.dot_general(q16, keys, NT, preferred_element_type=jnp.float32))
            length = jnp.where(row16 < 8, lens_ref[r], lens_ref[r + 1])
            valids.append(same & (position < length))
        maxima, totals, outs = [], [], []
        for i in range(PAIRS):
            r = base + 2 * i
            s = jnp.where(valids[i], scores[i] * scale, NEG_FILL)
            m = jnp.max(s, -1, keepdims=True)
            e = jnp.where(valids[i], jnp.exp(s - m), 0.0)
            maxima.append(m)
            totals.append(jnp.sum(e, -1, keepdims=True))
            values = jnp.concatenate(
                [cache_buf[g, r, :, head_dim:], cache_buf[g, r + 1, :, head_dim:]], 0
            )
            outs.append(
                jnp.dot(e.astype(jnp.bfloat16), values, preferred_element_type=jnp.float32)
            )
        return (
            start,
            jnp.concatenate(maxima, 0),
            jnp.concatenate(totals, 0),
            jnp.concatenate(outs, 0),
        )

    for g in range(heads):
        cache_copy(g).wait()

    def own_group(g, carry):
        for block in range(blocks):
            start, m, l, o = attend(query_ref, g, block)
            where = pl.ds(start, block_rows)
            own_out[where, :] = o
            own_max[where, :] = jnp.broadcast_to(m, (block_rows, 128))
            own_total[where, :] = jnp.broadcast_to(l, (block_rows, 128))
        return carry

    lax.fori_loop(0, heads, own_group, 0)

    def other_group(g, carry):
        query_copy(g).wait()
        for block in range(blocks):
            start, m, l, o = attend(other_query, g, block)
            back_buf[pl.ds(start, block_rows), :] = o.astype(jnp.bfloat16)
            at = pl.ds(g * blocks + block, 1)
            back_stats[0, at, :] = jnp.sum(jnp.where(eye, m, 0.0), 0, keepdims=True)
            back_stats[1, at, :] = jnp.sum(jnp.where(eye, l, 0.0), 0, keepdims=True)
        back_copy(g).start()
        return carry

    lax.fori_loop(0, heads, other_group, 0)
    stats_copy = pltpu.make_async_remote_copy(
        src_ref=back_stats,
        dst_ref=got_stats,
        send_sem=tail_send.at[0],
        recv_sem=tail_recv.at[0],
        device_id=partner,
        device_id_type=MESH,
    )
    stats_copy.start()

    for k in range(1, n_tp):
        sum_copy(k).wait()
    total = send_buf[tp].astype(jnp.float32)
    for k in range(1, n_tp):
        total += sum_buf[k].astype(jnp.float32)
    cosine, sine = cos_ref[...], sin_ref[...]
    for g in range(heads):
        x = total[:, g * head_dim : (g + 1) * head_dim]
        turned = x * cosine + pltpu.roll(x, head_dim // 2, 1) * sine
        piece_buf[:, g * head_dim : (g + 1) * head_dim] = jnp.where(upper == 0, turned, x).astype(
            jnp.bfloat16
        )
    piece_copy = pltpu.make_async_remote_copy(
        src_ref=piece_buf,
        dst_ref=other_piece,
        send_sem=tail_send.at[1],
        recv_sem=tail_recv.at[1],
        device_id=partner,
        device_id_type=MESH,
    )
    piece_copy.start()
    entries_ref[...] = piece_buf[...]
    piece_copy.wait()
    stats_copy.wait()

    q_row = lax.broadcasted_iota(jnp.int32, (block_rows, tokens), 0)
    k_col = lax.broadcasted_iota(jnp.int32, (block_rows, tokens), 1)
    for g in range(heads):
        cols = slice(g * head_dim, (g + 1) * head_dim)
        mine, theirs = piece_buf[:, cols], other_piece[:, cols]
        new_keys = jnp.where(upper == 0, mine, theirs)
        new_values = jnp.where(upper == 0, theirs, mine)
        back_copy(g).wait()
        for block in range(blocks):
            where = slice(g * group_rows + block * block_rows, g * group_rows + (block + 1) * block_rows)
            row_of = block * (block_rows // (2 * steps)) + q_row // (2 * steps)
            step_of = lax.rem(q_row, 2 * steps) // 2
            valid = (row_of == lax.rem(k_col, rows_dev)) & (k_col // rows_dev <= step_of)
            s = lax.dot_general(query_ref[where, :], new_keys, NT, preferred_element_type=jnp.float32)
            s = jnp.where(valid, s * scale, NEG_FILL)
            m3 = jnp.max(s, -1, keepdims=True)
            e = jnp.where(valid, jnp.exp(s - m3), 0.0)
            l3 = jnp.sum(e, -1, keepdims=True)
            o3 = jnp.dot(e.astype(jnp.bfloat16), new_values, preferred_element_type=jnp.float32)
            at = g * blocks + block
            m2 = jnp.sum(jnp.where(eye, got_stats[0, at : at + 1, :], 0.0), -1, keepdims=True)
            l2 = jnp.sum(jnp.where(eye, got_stats[1, at : at + 1, :], 0.0), -1, keepdims=True)
            m1, l1 = own_max[where, 0:1], own_total[where, 0:1]
            top = jnp.maximum(jnp.maximum(m1, m2), m3)
            f1, f2, f3 = jnp.exp(m1 - top), jnp.exp(m2 - top), jnp.exp(m3 - top)
            whole = own_out[where, :] * f1 + got_buf[where, :].astype(jnp.float32) * f2 + o3 * f3
            out_ref[where, :] = (whole / (l1 * f1 + l2 * f2 + l3 * f3)).astype(jnp.bfloat16)


def shards(
    sizes,
    hidden,
    w_kv,
    queries,
    cache,
    cache_lengths,
    updated,
    delta_values,
    delta_scales,
    delta_targets,
    send_counts,
):
    n_tp, n_pp, n_dp = sizes
    n_all = n_tp * n_pp * n_dp
    owners, slots, block_width = delta_values.shape[1:]
    shard_rows, width = w_kv.shape[1:]
    steps, rows_dev = hidden.shape[1:3]
    heads, half_positions = cache.shape[2:4]
    head_dim = cache.shape[4] // 2
    tokens = steps * rows_dev
    piece = width // n_tp
    all_queries = heads * rows_dev * steps * 2
    bf16, f32 = jnp.bfloat16, jnp.float32

    live = jnp.arange(slots, dtype=jnp.int32)[None, :] < send_counts[0][:, None]
    scales = jnp.where(live, delta_scales[0], jnp.zeros((), bf16))
    row_blocks = width // block_width
    target = delta_targets[0]
    row = target // row_blocks
    fields = (scales, (row // 16).astype(bf16), (row % 16).astype(bf16), (target % row_blocks).astype(bf16))
    lane = jnp.arange(block_width, dtype=jnp.int32)
    meta = jnp.zeros((owners, slots, block_width), bf16)
    for i, field in enumerate(fields):
        meta = jnp.where(lane == i, field[..., None], meta)
    packed = jnp.concatenate([delta_values[0], meta], 1).reshape(owners * 2 * slots, block_width)

    query_rows = queries[0].reshape(steps, rows_dev, heads, 2, head_dim)
    query_rows = query_rows.transpose(2, 1, 0, 3, 4).reshape(all_queries, head_dim)

    positions = cache_lengths[None, :] + jnp.arange(steps, dtype=jnp.int32)[:, None]
    half = head_dim // 2
    inverse = jnp.exp(
        jnp.arange(half).astype(f32) * (-2.0 / head_dim) * math.log(ROPE_BASE)
    )
    angles = positions.astype(f32).reshape(tokens, 1) * inverse
    cosine, sine = jnp.cos(angles), jnp.sin(angles)
    cosine = jnp.concatenate([cosine, cosine], 1)
    sine = jnp.concatenate([-sine, sine], 1)

    vmem = pl.BlockSpec(memory_space=pltpu.VMEM)
    anywhere = pl.BlockSpec(memory_space=pl.ANY)
    stat_rows = max(8, all_queries // 128)
    dma = pltpu.SemaphoreType.DMA
    entries, attended = pl.pallas_call(
        functools.partial(kernel, (n_tp, n_pp, n_dp, heads, rows_dev, steps)),
        out_shape=(
            jax.ShapeDtypeStruct((tokens, piece), bf16),
            jax.ShapeDtypeStruct((all_queries, head_dim), bf16),
        ),
        in_specs=[
            pl.BlockSpec(memory_space=pltpu.SMEM),
            vmem,
            anywhere,
            vmem,
            anywhere,
            vmem,
            vmem,
            vmem,
            vmem,
        ],
        out_specs=(vmem, vmem),
        scratch_shapes=[
            pltpu.VMEM((shard_rows, width), bf16),
            pltpu.VMEM((heads, rows_dev, half_positions, 2 * head_dim), bf16),
            pltpu.VMEM((n_all * 2 * slots, block_width), bf16),
            pltpu.VMEM((tokens, width), f32),
            pltpu.VMEM((n_tp, tokens, piece), bf16),
            pltpu.VMEM((n_tp, tokens, piece), bf16),
            pltpu.VMEM((tokens, piece), bf16),
            pltpu.VMEM((tokens, piece), bf16),
            pltpu.VMEM((all_queries, head_dim), bf16),
            pltpu.VMEM((all_queries, head_dim), bf16),
            pltpu.VMEM((2, stat_rows, 128), f32),
            pltpu.VMEM((all_queries, head_dim), bf16),
            pltpu.VMEM((2, stat_rows, 128), f32),
            pltpu.VMEM((all_queries, head_dim), f32),
            pltpu.VMEM((all_queries, 128), f32),
            pltpu.VMEM((all_queries, 128), f32),
            dma((2,)),
            dma((heads,)),
            dma((n_all,)),
            dma((n_all,)),
            dma((heads,)),
            dma((heads,)),
            dma((n_tp,)),
            dma((n_tp,)),
            dma((heads,)),
            dma((heads,)),
            dma((2,)),
            dma((2,)),
        ],
        compiler_params=pltpu.CompilerParams(
            collective_id=0, has_side_effects=True, vmem_limit_bytes=48 * 1024 * 1024
        ),
        name="decode",
    )(
        cache_lengths,
        hidden[0].reshape(tokens, shard_rows),
        w_kv[0],
        query_rows,
        cache[0],
        updated,
        packed,
        cosine,
        sine,
    )
    attended = attended.reshape(heads, rows_dev, steps, 2, head_dim).transpose(2, 1, 0, 3, 4)
    return (
        entries.reshape(1, steps, rows_dev, piece),
        attended.reshape(1, steps, rows_dev, heads * 2 * head_dim),
    )


def solution(mesh):
    placed = (
        P(("groups", "pp"), None, "dp", "tp"),
        P(("groups", "pp"), "tp", None),
        P(("groups", "pp"), None, "dp", "tp"),
        P(("groups", "pp"), "dp", "tp", None, None),
        P(("groups", "dp")),
        P(("groups", "pp"), "tp"),
        P(("groups", "tp", "pp", "dp"), None, None, None),
        P(("groups", "tp", "pp", "dp"), None, None),
        P(("groups", "tp", "pp", "dp"), None, None),
        P(("groups", "tp", "pp", "dp"), None),
    )
    sizes = (mesh.shape["tp"], mesh.shape["pp"], mesh.shape["dp"])
    return jax.shard_map(
        functools.partial(shards, sizes),
        mesh=mesh,
        in_specs=placed,
        out_specs=(P(("groups", "pp"), None, "dp", "tp"), P(("groups", "pp"), None, "dp", "tp")),
        check_vma=False,
    )
```

time: 504 us -> 64.3 us (0.13)
  waiting for transfers between devices: 397 us -> 0 us
  Pallas kernels: 0 us -> 54.4 us
  matrix products: 25.9 us -> 0 us
  other arithmetic: 24.1 us -> 3.37 us
  starting transfers between devices: 16.2 us -> 0 us
  local copies, waits for them, and re-layouts: 19.9 us -> 5.41 us
  between operations: 14.3 us -> 0.71 us
  blocking collectives: 5.39 us -> 0 us
    all_to_all x3 -> x0, waiting for transfers between devices: 362 us -> none  [the longest x1 354 us: shards(): lax.all_to_all(sent_scales, ('tp', 'pp'), split_axis=0, concat_axis=0, ti...]
    pallas_call x0 -> x1, Pallas kernels: none -> 54.4 us  [shards(): pl.pallas_call(functools.partial(kernel, (n_tp, n_pp, n_dp, heads, rows_d...]
    psum x1 -> x0, waiting for transfers between devices: 35.7 us -> none  [shards(): lax.psum(jnp.dot(flat_rows, weight, preferred_element_type=jnp.float32).a...]
    dot_general x5 -> x0, matrix products: 25.9 us -> none  [the longest x1 10.1 us: shards(): jnp.dot(flat_rows, weight, preferred_element_type=jnp.float32)]
    reshape x4 -> x1, local copies, waits for them, and re-layouts: 13.2 us -> 0.87 us  [shards(): attended.reshape(1, steps, rows_dev, heads * 2 * head_dim)]
    all_to_all x3 -> x0, starting transfers between devices: 12 us -> none  [the longest x1 4.89 us: shards(): lax.all_to_all(delta_targets[0], ('tp', 'pp'), split_axis=0, concat_axis=...]
    select_n x3 -> x2, other arithmetic: 12.1 us -> 0.86 us  [the longest x1 0.76 us: shards(): scales = jnp.where(live, delta_scales[0], jnp.zeros((), bf16))]
    scatter-add x1 -> x0, other arithmetic: 5.62 us -> none  [shards(): dense_delta.at[all_targets.reshape(-1)]]
  transfers between devices with their start and end apart: 5 -> 0, of which waited for: 4 -> 0; matrix products, arithmetic and copies ran while one was open for 8% -> 0% of each run, Pallas kernels for 0% -> 0%
where the time goes in v1:
time: 64.3 us; the launch traced here: 63.9 us
  Pallas kernels  54.4 us (85%)
  local copies, waits for them, and re-layouts  5.41 us (8%)
  other arithmetic  3.37 us (5%)
  between operations  0.71 us (1%)
    pallas_call x1, Pallas kernels, shards(): pl.pallas_call(functools.partial(kernel, (n_tp, n_pp, n_dp, heads, rows_d...  54.4 us
    unnamed x7, local copies, waits for them, and re-layouts  2.97 us
    another operation x2, local copies, waits for them, and re-layouts, shards(): query_rows = queries[0].reshape(steps, rows_dev, heads, 2, head_dim)  1.3 us

profile of v1, /device:TPU:0, one launch (start us, length us, event | category | flops | bytes accessed | tf_op | source)
XLA Modules:
  0.0 63.9 jit_solution(1666846363949303927)
XLA Ops:
  0.7 0.8 %fusion.6 = bf16[8,8]{1,0:T(8,128)(2,1)S(1)} fusion(bf16[1,8,8]{2,1,0:T(8,128)(2,1)} %param.17, s32[8]{0:T(128)} %bitcast.55), kind=kLoop, calls=%fused_computation.26 | loop fusion | flops 128 | bytes 288 | tf_op jit(solution)/shard_map/jit(_where)/select_n | solution.py:372
  1.4 0.7 %add_convert_fusion = f32[4,32]{1,0:T(4,128)S(1)} fusion(s32[32]{0:T(128)} %lens_ref.1), kind=kLoop, calls=%fused_computation.30 | loop fusion | flops 256 | bytes 640 | tf_op jit(solution)/shard_map/convert_element_type | solution.py:391
  2.1 0.1 convert_element_type.42
  2.2 0.7 %fusion.1 = (bf16[8,8]{1,0:T(8,128)(2,1)S(1)}, bf16[8,8]{1,0:T(8,128)(2,1)S(1)}, bf16[8,8]{1,0:T(8,128)(2,1)S(1)}) fusion(s32[1,8,8]{2,1,0:T(8,128)} %param.18), kind=kLoop, calls=%fused_computation.17 | loop fusion | flops 2624 | bytes 640 | tf_op jit(solution)/shard_map/convert_element_type | solution.py:376
  2.9 0.1 select_select_fusion
  3.0 0.7 %pad_maximum_fusion.2 = bf16[8,16,128]{2,1,0:T(8,128)(2,1)S(1)} fusion(bf16[8,8,128]{2,1,0:T(8,128)(2,1)S(1)} %select_select_fusion, bf16[8,8,128]{2,1,0:T(8,128)(2,1)} %bitcast.54), kind=kLoop, calls=%fused_computation.4 | loop fusion | flops 65536 | bytes 65536 | tf_op jit(solution)/shard_map/concatenate | solution.py:381
  3.7 0.3 fusion
  4.0 0.1 pad_maximum_fusion
  4.1 1.1 %reshape_squeeze.7 = bf16[4,32,4,2,128]{4,3,2,1,0:T(2,128)(2,1)S(1)} reshape(bf16[1,4,32,1024]{3,2,1,0:T(8,128)(2,1)} %param.12) | data formatting | bytes 524288 | tf_op jit(solution)/shard_map/reshape;squeeze | solution.py:383
  5.3 0.2 copy.12
  5.4 0.0 copy-start
  5.5 1.0 %copy-done = bf16[1,4,32,1280]{3,2,1,0:T(8,128)(2,1)S(1)} copy-done((bf16[1,4,32,1280]{3,2,1,0:T(8,128)(2,1)S(1)}, bf16[1,4,32,1280]{3,2,1,0:T(8,128)(2,1)}, u32[]{:S(2)}) %copy-start) | copy-done | bytes 327704
  6.4 0.0 copy-start.1
  6.4 0.7 %copy-done.1 = s32[1,1280]{1,0:T(1,128)S(1)} copy-done((s32[1,1280]{1,0:T(1,128)S(1)}, s32[1,1280]{1,0:T(1,128)}, u32[]{:S(2)}) %copy-start.1) | copy-done | bytes 5144
  7.1 0.0 copy-start.2
  7.1 0.7 %copy-done.2 = s32[32]{0:T(128)S(1)} copy-done((s32[32]{0:T(128)S(1)}, s32[32]{0:T(128)}, u32[]{:S(2)}) %copy-start.2) | copy-done | bytes 152
  7.8 54.4 %decode.1 = (bf16[128,512]{1,0:T(8,128)(2,1)S(1)}, bf16[1024,128]{1,0:T(8,128)(2,1)S(1)}) custom-call(s32[32]{0:T(128)S(1)} %copy-done.2, bf16[128,1280]{1,0:T(8,128)(2,1)S(1)} %bitcast.48, bf16[1280,2048]{1,0:T(8,128)(2,1)} %bitcast.53, bf16[1024,128]{1,0:T(8,128)(2,1)S(1)} %bitcast.47, bf16[32,4,128,256]{3,2,1,0:T(8,128)(2,1)} %bitcast.52, ...), custom_call_target="tpu_custom_call" | custom-call | tf_op jit(solution)/shard_map/decode/pallas_call | solution.py:400
  62.1 0.2 copy.13
  62.3 0.9 %reshape.163 = bf16[1,4,32,1024]{3,2,1,0:T(8,128)(2,1)} reshape(bf16[4,32,4,2,128]{4,3,2,1,0:T(2,128)(2,1)S(1)} %copy.13) | data formatting | bytes 524288 | tf_op jit(solution)/shard_map/reshape | solution.py:466
  63.2 0.7 %copy.15 = bf16[1,4,32,512]{3,2,1,0:T(8,128)(2,1)} copy(bf16[1,4,32,512]{3,2,1,0:T(8,128)(2,1)S(1)} %bitcast.51) | data formatting | bytes 262144
  (3 shorter events, 0.0 us)
Async XLA Ops:
  5.4 1.0 %copy-start = (bf16[1,4,32,1280]{3,2,1,0:T(8,128)(2,1)S(1)}, bf16[1,4,32,1280]{3,2,1,0:T(8,128)(2,1)}, u32[]{:S(2)}) copy-start(bf16[1,4,32,1280]{3,2,1,0:T(8,128)(2,1)} %param.10) | copy-start | bytes 983044
  6.4 0.7 %copy-start.1 = (s32[1,1280]{1,0:T(1,128)S(1)}, s32[1,1280]{1,0:T(1,128)}, u32[]{:S(2)}) copy-start(s32[1,1280]{1,0:T(1,128)} %updated_ref.1) | copy-start | bytes 15364
  7.1 0.7 %copy-start.2 = (s32[32]{0:T(128)S(1)}, s32[32]{0:T(128)}, u32[]{:S(2)}) copy-start(s32[32]{0:T(128)} %lens_ref.1) | copy-start | bytes 388

commit v2 on v1

v2 whole, which is shorter than its diff:
```python
import functools
import math

import jax
import jax.numpy as jnp
from jax import lax
from jax.experimental import pallas as pl
from jax.experimental.pallas import tpu as pltpu
from jax.sharding import PartitionSpec as P

ROPE_BASE = 1000000.0
NEG_FILL = -1e30
MESH = pl.DeviceIdType.MESH
NT = (((1,), (1,)), ((), ()))
PAIRS = 8


def kernel(
    dims,
    lens_hbm,
    hidden_hbm,
    w_hbm,
    query_hbm,
    cache_hbm,
    updated_hbm,
    values_hbm,
    scales_hbm,
    targets_hbm,
    counts_hbm,
    entries_ref,
    out_ref,
    lens_ref,
    lens_row,
    hidden_ref,
    w_buf,
    query_raw,
    cache_buf,
    updated_ref,
    values_ref,
    scales_ref,
    targets_ref,
    counts_ref,
    scales_wide,
    packed_ref,
    query_wide,
    query_ref,
    cos_ref,
    sin_ref,
    delta_buf,
    product,
    send_buf,
    sum_buf,
    pair_buf,
    pair_got,
    kept_sum,
    piece_buf,
    other_piece,
    other_query,
    back_buf,
    back_stats,
    got_buf,
    got_stats,
    own_out,
    own_max,
    own_total,
    local_sem,
    cache_sem,
    delta_send,
    delta_recv,
    query_send,
    query_recv,
    sum_send,
    sum_recv,
    back_send,
    back_recv,
    tail_send,
    tail_recv,
):
    n_tp, n_pp, n_dp, row_blocks = dims
    n_all = n_tp * n_pp * n_dp
    n_half = n_tp // 2
    heads, rows_dev, half_positions, head_dim = cache_buf.shape
    head_dim = head_dim // 2
    tokens, width = product.shape
    steps = tokens // rows_dev
    owners, slots = targets_ref.shape
    piece = width // n_tp
    row_queries = 2 * steps
    group_rows = rows_dev * row_queries
    blocks = group_rows // (16 * PAIRS)
    block_rows = 16 * PAIRS
    slot_rows = 16
    tp = lax.axis_index("tp")
    me = (tp * n_pp + lax.axis_index("pp")) * n_dp + lax.axis_index("dp")
    upper = tp // n_half
    place_in_half = lax.rem(tp, n_half)
    partner = {"tp": lax.rem(tp + n_half, n_tp)}
    scale = 1.0 / math.sqrt(head_dim)
    f32, bf16 = jnp.float32, jnp.bfloat16

    def load(i, source, target):
        copy = pltpu.make_async_copy(source, target, local_sem.at[i])
        copy.start()
        return copy

    small = [
        load(2, scales_hbm, scales_ref),
        load(3, targets_hbm, targets_ref),
        load(4, counts_hbm, counts_ref),
        load(5, values_hbm, values_ref),
    ]
    query_load = load(6, query_hbm, query_raw)
    hidden_load = load(7, hidden_hbm, hidden_ref)
    later = [
        load(8, updated_hbm, updated_ref),
        load(9, lens_hbm, lens_ref),
        load(10, lens_hbm, lens_row),
    ]
    w_copy = load(0, w_hbm, w_buf)

    def cache_copy(g):
        return pltpu.make_async_copy(cache_hbm.at[:, g], cache_buf.at[g], cache_sem.at[g])

    for g in range(heads):
        cache_copy(g).start()

    def place(index):
        return {
            "tp": index // (n_pp * n_dp),
            "pp": lax.rem(index // n_dp, n_pp),
            "dp": lax.rem(index, n_dp),
        }

    barrier = pltpu.get_barrier_semaphore()

    def greet(k, carry):
        pl.semaphore_signal(
            barrier, inc=1, device_id=place(lax.rem(me + k, n_all)), device_id_type=MESH
        )
        return carry

    lax.fori_loop(1, n_all, greet, 0)

    query_load.wait()
    for g in range(heads):
        for t in range(steps):
            for b in range(2):
                lanes = slice((g * 2 + b) * head_dim, (g * 2 + b + 1) * head_dim)
                query_wide[pl.ds(g * group_rows + t * 2 + b, rows_dev, stride=row_queries), :] = (
                    query_raw[t, :, lanes].astype(f32)
                )
    query_ref[...] = query_wide[...].astype(bf16)

    for copy in small:
        copy.wait()
    scales_wide[...] = scales_ref[...].astype(f32)
    row8 = lax.broadcasted_iota(jnp.int32, (slots, slots), 0)
    col8 = lax.broadcasted_iota(jnp.int32, (slots, slots), 1)
    lane = lax.broadcasted_iota(jnp.int32, (slots, 128), 1)
    owner_lane = lax.broadcasted_iota(jnp.int32, counts_ref.shape, 1)

    def pack(o, carry):
        def column(x):
            wide = jnp.where(row8 == col8, jnp.broadcast_to(x, (slots, slots)), 0.0)
            return jnp.sum(wide, -1, keepdims=True)

        count = jnp.sum(jnp.where(owner_lane == o, counts_ref[...].astype(f32), 0.0), -1, keepdims=True)
        scales = scales_wide[pl.ds(o, 1), :]
        scales = jnp.where(col8[:1].astype(f32) < count, scales, 0.0)
        target = targets_ref[pl.ds(o, 1), :]
        shift = row_blocks.bit_length() - 1
        high = (target >> (shift + 4)).astype(f32)
        low = ((target >> shift) & 15).astype(f32)
        block = (target & (row_blocks - 1)).astype(f32)
        meta = jnp.zeros((slots, 128), f32)
        for i, field in enumerate((scales, high, low, block)):
            meta = jnp.where(lane == i, column(field), meta)
        both = jnp.concatenate([values_ref[o].astype(f32), meta], 0)
        packed_ref[pl.ds(pl.multiple_of(o * slot_rows, slot_rows), slot_rows), :] = both.astype(bf16)
        return carry

    lax.fori_loop(0, owners, pack, 0)
    pl.semaphore_wait(barrier, n_all - 1)

    def owner_rows(index):
        return pl.ds(pl.multiple_of((index // n_dp) * slot_rows, slot_rows), slot_rows)

    my_rows = pl.ds(pl.multiple_of(me * slot_rows, slot_rows), slot_rows)

    def delta_copy(k):
        target = lax.rem(me + k, n_all)
        return pltpu.make_async_remote_copy(
            src_ref=packed_ref.at[owner_rows(target)],
            dst_ref=delta_buf.at[my_rows],
            send_sem=delta_send.at[k],
            recv_sem=delta_recv.at[k],
            device_id=place(target),
            device_id_type=MESH,
        )

    def group_slice(g):
        return pl.ds(pl.multiple_of(g * group_rows, group_rows), group_rows)

    def query_copy(g):
        return pltpu.make_async_remote_copy(
            src_ref=query_ref.at[group_slice(g)],
            dst_ref=other_query.at[group_slice(g)],
            send_sem=query_send.at[g],
            recv_sem=query_recv.at[g],
            device_id=partner,
            device_id_type=MESH,
        )

    def back_copy(g):
        return pltpu.make_async_remote_copy(
            src_ref=back_buf.at[group_slice(g)],
            dst_ref=got_buf.at[group_slice(g)],
            send_sem=back_send.at[g],
            recv_sem=back_recv.at[g],
            device_id=partner,
            device_id_type=MESH,
        )

    def start_delta(k, carry):
        delta_copy(k).start()
        return carry

    query_copy(0).start()
    lax.fori_loop(1, n_all, start_delta, 0)
    own_delta = pltpu.make_async_copy(
        packed_ref.at[owner_rows(me)], delta_buf.at[my_rows], local_sem.at[1]
    )
    own_delta.start()
    for g in range(1, heads):
        query_copy(g).start()

    hidden_load.wait()
    hidden = hidden_ref[...]
    w_copy.wait()
    tile = 256
    for c in range(width // tile):
        cols = slice(c * tile, (c + 1) * tile)
        product[:, cols] = jnp.dot(hidden, w_buf[:, cols], preferred_element_type=f32)

    for copy in later:
        copy.wait()

    def wait_delta(k, carry):
        delta_copy(k).wait()
        return carry

    lax.fori_loop(1, n_all, wait_delta, 0)
    own_delta.wait()
    shard_rows = hidden.shape[1]
    row_index = lax.broadcasted_iota(jnp.int32, (128, shard_rows), 1).astype(f32)
    taken = jnp.broadcast_to(updated_ref[...], (128, shard_rows)) == 1

    def add_deltas(chunk, carry):
        got = delta_buf[pl.ds(pl.multiple_of(chunk * 256, 256), 256), :].astype(f32)
        got = got.reshape(16, 16, 128)
        values = got[:, :8].reshape(128, 128)
        meta = got[:, 8:].reshape(128, 128)
        row = meta[:, 1:2] * 16.0 + meta[:, 2:3]
        place_row = jnp.where((row_index == row) & taken, meta[:, 0:1], 0.0).astype(bf16)
        picked = lax.dot_general(hidden, place_row, NT, preferred_element_type=f32)
        high = picked.astype(bf16)
        low = (picked - high.astype(f32)).astype(bf16)
        for c in range(width // tile):
            cols = slice(c * tile, (c + 1) * tile)
            spread = jnp.concatenate(
                [
                    jnp.where(meta[:, 3:4] == float(j), values, 0.0)
                    for j in range(c * tile // 128, (c + 1) * tile // 128)
                ],
                1,
            ).astype(bf16)
            product[:, cols] += jnp.dot(high, spread, preferred_element_type=f32) + jnp.dot(
                low, spread, preferred_element_type=f32
            )
        return carry

    lax.fori_loop(0, n_all // 16, add_deltas, 0)
    for j in range(n_half):
        for part in range(2):
            i = part * n_half + j
            send_buf[j, part] = product[:, i * piece : (i + 1) * piece].astype(bf16)

    def sum_copy(k):
        target = lax.rem(place_in_half + k, n_half)
        return pltpu.make_async_remote_copy(
            src_ref=send_buf.at[target],
            dst_ref=sum_buf.at[k],
            send_sem=sum_send.at[k],
            recv_sem=sum_recv.at[k],
            device_id={"tp": upper * n_half + target},
            device_id_type=MESH,
        )

    for k in range(1, n_half):
        sum_copy(k).start()

    def tail_copy(i, source, target):
        return pltpu.make_async_remote_copy(
            src_ref=source,
            dst_ref=target,
            send_sem=tail_send.at[i],
            recv_sem=tail_recv.at[i],
            device_id=partner,
            device_id_type=MESH,
        )

    row16 = lax.broadcasted_iota(jnp.int32, (16, 256), 0)
    col16 = lax.broadcasted_iota(jnp.int32, (16, 256), 1)
    same = (row16 // 8) == (col16 // 128)
    position = lax.rem(col16, 128) + upper * half_positions
    eye = lax.broadcasted_iota(jnp.int32, (128, 128), 0) == lax.broadcasted_iota(
        jnp.int32, (128, 128), 1
    )

    def attend(source, g, block):
        base = block * 2 * PAIRS
        scores, valids = [], []
        start = pl.multiple_of(g * group_rows + block * block_rows, block_rows)
        for i in range(PAIRS):
            r = base + 2 * i
            keys = jnp.concatenate(
                [cache_buf[g, r, :, :head_dim], cache_buf[g, r + 1, :, :head_dim]], 0
            )
            q16 = source[pl.ds(start + 16 * i, 16), :]
            scores.append(lax.dot_general(q16, keys, NT, preferred_element_type=f32))
            length = jnp.where(row16 < 8, lens_ref[r], lens_ref[r + 1])
            valids.append(same & (position < length))
        maxima, totals, outs = [], [], []
        for i in range(PAIRS):
            r = base + 2 * i
            s = jnp.where(valids[i], scores[i] * scale, NEG_FILL)
            m = jnp.max(s, -1, keepdims=True)
            e = jnp.where(valids[i], jnp.exp(s - m), 0.0)
            maxima.append(m)
            totals.append(jnp.sum(e, -1, keepdims=True))
            values = jnp.concatenate(
                [cache_buf[g, r, :, head_dim:], cache_buf[g, r + 1, :, head_dim:]], 0
            )
            outs.append(jnp.dot(e.astype(bf16), values, preferred_element_type=f32))
        return (
            start,
            jnp.concatenate(maxima, 0),
            jnp.concatenate(totals, 0),
            jnp.concatenate(outs, 0),
        )

    def other_group(g, carry):
        cache_copy(g).wait()
        query_copy(g).wait()
        for block in range(blocks):
            start, m, l, o = attend(other_query, g, block)
            back_buf[pl.ds(start, block_rows), :] = o.astype(bf16)
            at = pl.ds(g * blocks + block, 1)
            back_stats[0, at, :] = jnp.sum(jnp.where(eye, m, 0.0), 0, keepdims=True)
            back_stats[1, at, :] = jnp.sum(jnp.where(eye, l, 0.0), 0, keepdims=True)
        back_copy(g).start()
        return carry

    to_column = lax.broadcasted_iota(jnp.int32, (rows_dev, rows_dev), 0) == lax.broadcasted_iota(
        jnp.int32, (rows_dev, rows_dev), 1
    )
    lengths = jnp.broadcast_to(lens_row[...].astype(f32).reshape(1, rows_dev), (rows_dev, rows_dev))
    lengths = jnp.sum(jnp.where(to_column, lengths, 0.0), -1, keepdims=True)
    index = lax.rem(lax.broadcasted_iota(jnp.int32, (1, head_dim), 1), head_dim // 2).astype(f32)
    inverse = jnp.exp(index * (-2.0 / head_dim) * math.log(ROPE_BASE))
    positions = jnp.concatenate([lengths + float(t) for t in range(steps)], 0)
    angles = positions * inverse
    first = lax.broadcasted_iota(jnp.int32, (tokens, head_dim), 1) < head_dim // 2
    sine = jnp.sin(angles)
    cos_ref[...] = jnp.cos(angles)
    sin_ref[...] = jnp.where(first, -sine, sine)

    early = (heads + 1) // 2
    lax.fori_loop(0, early, other_group, 0)

    for k in range(1, n_half):
        sum_copy(k).wait()
    sums = []
    for part in range(2):
        total = send_buf[place_in_half, part].astype(f32)
        for k in range(1, n_half):
            total += sum_buf[k, part].astype(f32)
        sums.append(total)
    kept_sum[...] = jnp.where(upper == 0, sums[0], sums[1])
    pair_buf[...] = jnp.where(upper == 0, sums[1], sums[0]).astype(bf16)
    pair_copy = tail_copy(2, pair_buf, pair_got)
    pair_copy.start()

    lax.fori_loop(early, heads, other_group, 0)
    stats_copy = tail_copy(0, back_stats, got_stats)
    stats_copy.start()

    pair_copy.wait()
    for g in range(heads):
        cols = slice(g * head_dim, (g + 1) * head_dim)
        x = kept_sum[:, cols] + pair_got[:, cols].astype(f32)
        turned = x * cos_ref[...] + pltpu.roll(x, head_dim // 2, 1) * sin_ref[...]
        piece_buf[:, cols] = jnp.where(upper == 0, turned, x).astype(bf16)
    piece_copy = tail_copy(1, piece_buf, other_piece)
    piece_copy.start()
    entries_ref[...] = piece_buf[...]

    def own_group(g, carry):
        for block in range(blocks):
            start, m, l, o = attend(query_ref, g, block)
            where = pl.ds(start, block_rows)
            own_out[where, :] = o
            own_max[where, :] = jnp.broadcast_to(m, (block_rows, 128))
            own_total[where, :] = jnp.broadcast_to(l, (block_rows, 128))
        return carry

    lax.fori_loop(0, heads, own_group, 0)
    piece_copy.wait()

    q_row = lax.broadcasted_iota(jnp.int32, (block_rows, tokens), 0)
    k_col = lax.broadcasted_iota(jnp.int32, (block_rows, tokens), 1)
    step_of = lax.rem(q_row, row_queries) // 2
    seen = k_col // rows_dev <= step_of
    for g in range(heads):
        cols = slice(g * head_dim, (g + 1) * head_dim)
        mine, theirs = piece_buf[:, cols], other_piece[:, cols]
        new_keys = jnp.where(upper == 0, mine, theirs)
        new_values = jnp.where(upper == 0, theirs, mine)
        for block in range(blocks):
            first_row = g * group_rows + block * block_rows
            where = slice(first_row, first_row + block_rows)
            row_of = block * (block_rows // row_queries) + q_row // row_queries
            valid = (row_of == lax.rem(k_col, rows_dev)) & seen
            s = lax.dot_general(query_ref[where, :], new_keys, NT, preferred_element_type=f32)
            s = jnp.where(valid, s * scale, NEG_FILL)
            m1, l1 = own_max[where, :], own_total[where, :]
            top = jnp.maximum(jnp.max(s, -1, keepdims=True), m1)
            e = jnp.where(valid, jnp.exp(s - top), 0.0)
            o3 = jnp.dot(e.astype(bf16), new_values, preferred_element_type=f32)
            f1 = jnp.exp(m1 - top)
            own_out[where, :] = own_out[where, :] * f1 + o3
            own_total[where, :] = l1 * f1 + jnp.sum(e, -1, keepdims=True)
            own_max[where, :] = top

    stats_copy.wait()
    for g in range(heads):
        back_copy(g).wait()
        for block in range(blocks):
            first_row = g * group_rows + block * block_rows
            where = slice(first_row, first_row + block_rows)
            at = g * blocks + block
            m2 = jnp.sum(jnp.where(eye, got_stats[0, at : at + 1, :], 0.0), -1, keepdims=True)
            l2 = jnp.sum(jnp.where(eye, got_stats[1, at : at + 1, :], 0.0), -1, keepdims=True)
            m1 = own_max[where, :]
            top = jnp.maximum(m1, m2)
            f1, f2 = jnp.exp(m1 - top), jnp.exp(m2 - top)
            whole = own_out[where, :] * f1 + got_buf[where, :].astype(f32) * f2
            query_wide[where, :] = whole / (own_total[where, :] * f1 + l2 * f2)
        for t in range(steps):
            for b in range(2):
                lanes = slice((g * 2 + b) * head_dim, (g * 2 + b + 1) * head_dim)
                rows = pl.ds(g * group_rows + t * 2 + b, rows_dev, stride=row_queries)
                out_ref[t, :, lanes] = query_wide[rows, :].astype(bf16)


def shards(
    sizes,
    hidden,
    w_kv,
    queries,
    cache,
    cache_lengths,
    updated,
    delta_values,
    delta_scales,
    delta_targets,
    send_counts,
):
    n_tp, n_pp, n_dp = sizes
    n_all = n_tp * n_pp * n_dp
    owners, slots, block_width = delta_values.shape[1:]
    shard_rows, width = w_kv.shape[1:]
    steps, rows_dev = hidden.shape[1:3]
    heads, half_positions = cache.shape[2:4]
    head_dim = cache.shape[4] // 2
    tokens = steps * rows_dev
    piece = width // n_tp
    all_queries = heads * rows_dev * steps * 2
    bf16, f32, i32 = jnp.bfloat16, jnp.float32, jnp.int32

    vmem = pl.BlockSpec(memory_space=pltpu.VMEM)
    anywhere = pl.BlockSpec(memory_space=pl.ANY)
    stat_rows = max(8, all_queries // 128)
    dma = pltpu.SemaphoreType.DMA
    rows = pltpu.VMEM((all_queries, head_dim), bf16)
    wide_rows = pltpu.VMEM((all_queries, head_dim), f32)
    stats = pltpu.VMEM((2, stat_rows, 128), f32)
    one_piece = pltpu.VMEM((tokens, piece), bf16)
    table = pltpu.VMEM((tokens, head_dim), f32)
    entries, attended = pl.pallas_call(
        functools.partial(kernel, (n_tp, n_pp, n_dp, width // block_width)),
        out_shape=(
            jax.ShapeDtypeStruct((tokens, piece), bf16),
            jax.ShapeDtypeStruct((steps, rows_dev, heads * 2 * head_dim), bf16),
        ),
        in_specs=[anywhere] * 10,
        out_specs=(vmem, vmem),
        scratch_shapes=[
            pltpu.SMEM((rows_dev,), i32),
            pltpu.VMEM((rows_dev,), i32),
            pltpu.VMEM((tokens, shard_rows), bf16),
            pltpu.VMEM((shard_rows, width), bf16),
            pltpu.VMEM((steps, rows_dev, heads * 2 * head_dim), bf16),
            pltpu.VMEM((heads, rows_dev, half_positions, 2 * head_dim), bf16),
            pltpu.VMEM((1, shard_rows), i32),
            pltpu.VMEM((owners, slots, block_width), bf16),
            pltpu.VMEM((owners, slots), bf16),
            pltpu.VMEM((owners, slots), i32),
            pltpu.VMEM((1, owners), i32),
            pltpu.VMEM((owners, slots), f32),
            pltpu.VMEM((owners * 2 * slots, block_width), bf16),
            wide_rows,
            rows,
            table,
            table,
            pltpu.VMEM((n_all * 2 * slots, block_width), bf16),
            pltpu.VMEM((tokens, width), f32),
            pltpu.VMEM((n_tp // 2, 2, tokens, piece), bf16),
            pltpu.VMEM((n_tp // 2, 2, tokens, piece), bf16),
            one_piece,
            one_piece,
            pltpu.VMEM((tokens, piece), f32),
            one_piece,
            one_piece,
            rows,
            rows,
            stats,
            rows,
            stats,
            wide_rows,
            wide_rows,
            wide_rows,
            dma((11,)),
            dma((heads,)),
            dma((n_all,)),
            dma((n_all,)),
            dma((heads,)),
            dma((heads,)),
            dma((n_tp // 2,)),
            dma((n_tp // 2,)),
            dma((heads,)),
            dma((heads,)),
            dma((3,)),
            dma((3,)),
        ],
        compiler_params=pltpu.CompilerParams(
            collective_id=0, has_side_effects=True, vmem_limit_bytes=56 * 1024 * 1024
        ),
        name="decode",
    )(
        cache_lengths,
        hidden[0].reshape(tokens, shard_rows),
        w_kv[0],
        queries[0],
        cache[0],
        updated,
        delta_values[0],
        delta_scales[0],
        delta_targets[0],
        send_counts,
    )
    return (entries.reshape(1, steps, rows_dev, piece), attended[None])


def solution(mesh):
    placed = (
        P(("groups", "pp"), None, "dp", "tp"),
        P(("groups", "pp"), "tp", None),
        P(("groups", "pp"), None, "dp", "tp"),
        P(("groups", "pp"), "dp", "tp", None, None),
        P(("groups", "dp")),
        P(("groups", "pp"), "tp"),
        P(("groups", "tp", "pp", "dp"), None, None, None),
        P(("groups", "tp", "pp", "dp"), None, None),
        P(("groups", "tp", "pp", "dp"), None, None),
        P(("groups", "tp", "pp", "dp"), None),
    )
    sizes = (mesh.shape["tp"], mesh.shape["pp"], mesh.shape["dp"])
    return jax.shard_map(
        functools.partial(shards, sizes),
        mesh=mesh,
        in_specs=placed,
        out_specs=(P(("groups", "pp"), None, "dp", "tp"), P(("groups", "pp"), None, "dp", "tp")),
        check_vma=False,
    )
```

time: 64.3 us -> 55.6 us (0.86)
  other arithmetic: 3.37 us -> 0 us
  Pallas kernels: 54.4 us -> 51.5 us
  local copies, waits for them, and re-layouts: 5.41 us -> 3.24 us
    pallas_call x1, Pallas kernels: 54.4 us -> 51.5 us  [shards(): pl.pallas_call(functools.partial(kernel, (n_tp, n_pp, n_dp, width // bloc...]
    convert_element_type x2 -> x0, other arithmetic: 1.37 us -> none  [the longest x1 0.71 us: shards(): (target % row_blocks).astype(bf16)]
    another operation x2 -> x0, local copies, waits for them, and re-layouts: 1.3 us -> none  [shards(): query_rows = queries[0].reshape(steps, rows_dev, heads, 2, head_dim)]
    reshape x1 -> x0, local copies, waits for them, and re-layouts: 0.87 us -> none  [shards(): attended.reshape(1, steps, rows_dev, heads * 2 * head_dim)]
    select_n x2 -> x0, other arithmetic: 0.86 us -> none  [the longest x1 0.76 us: shards(): scales = jnp.where(live, delta_scales[0], jnp.zeros((), bf16))]
    concatenate x2 -> x0, other arithmetic: 0.83 us -> none  [the longest x1 0.73 us: shards(): jnp.concatenate([delta_values[0], meta], 1)]
    unnamed x7 -> x2, local copies, waits for them, and re-layouts: 2.97 us -> 3.24 us
where the time goes in v2:
time: 55.6 us; the launch traced here: 55.4 us
  Pallas kernels  51.5 us (93%)
  local copies, waits for them, and re-layouts  3.24 us (6%)
  between operations  0.64 us (1%)
    pallas_call x1, Pallas kernels, shards(): pl.pallas_call(functools.partial(kernel, (n_tp, n_pp, n_dp, width // bloc...  51.5 us
    unnamed x2, local copies, waits for them, and re-layouts  3.24 us

profile of v2, /device:TPU:0, one launch (start us, length us, event | category | flops | bytes accessed | tf_op | source)
XLA Modules:
  0.0 55.4 jit_solution(2956516753797483605)
XLA Ops:
  0.6 51.5 %decode.1 = (bf16[128,512]{1,0:T(8,128)(2,1)}, bf16[4,32,1024]{2,1,0:T(8,128)(2,1)}) custom-call(s32[32]{0:T(128)} %lens_hbm.1, bf16[128,1280]{1,0:T(8,128)(2,1)} %bitcast.11, bf16[1280,2048]{1,0:T(8,128)(2,1)} %bitcast.10, bf16[4,32,1024]{2,1,0:T(8,128)(2,1)} %bitcast.12, bf16[32,4,128,256]{3,2,1,0:T(8,128)(2,1)} %bitcast.9, s32[1,1280]{1,0:T(1,128)} %updated_hbm.1, ...), custom_call_target="tpu_custom_call" | custom-call | tf_op jit(solution)/shard_map/decode/pallas_call | solution.py:500
  52.2 1.6 %copy.14 = bf16[1,4,32,512]{3,2,1,0:T(8,128)(2,1)} copy(bf16[1,4,32,512]{3,2,1,0:T(8,128)(2,1)} %bitcast.14) | data formatting | bytes 262144
  53.8 1.7 %copy.15 = bf16[1,4,32,1024]{3,2,1,0:T(8,128)(2,1)} copy(bf16[1,4,32,1024]{3,2,1,0:T(8,128)(2,1)} %bitcast.13) | data formatting | bytes 524288

commit v3 on v2

--- a/solution.py
+++ b/solution.py
@@ -225,13 +225,12 @@
         delta_copy(k).start()
         return carry
 
-    query_copy(0).start()
     lax.fori_loop(1, n_all, start_delta, 0)
     own_delta = pltpu.make_async_copy(
         packed_ref.at[owner_rows(me)], delta_buf.at[my_rows], local_sem.at[1]
     )
     own_delta.start()
-    for g in range(1, heads):
+    for g in range(heads):
         query_copy(g).start()
 
     hidden_load.wait()

time: 55.6 us -> 52.6 us (0.946)
  the two profiles are of different devices: /device:TPU:0 before, /device:TPU:10 now
where the time goes in v3:
time: 52.6 us; the launch traced here: 52.5 us
  Pallas kernels  48.6 us (92%)
  local copies, waits for them, and re-layouts  3.24 us (6%)
  between operations  0.64 us (1%)
    pallas_call x1, Pallas kernels, shards(): pl.pallas_call(functools.partial(kernel, (n_tp, n_pp, n_dp, width // bloc...  48.6 us
    unnamed x2, local copies, waits for them, and re-layouts  3.24 us

profile of v3, /device:TPU:10, one launch (start us, length us, event | category | flops | bytes accessed | tf_op | source)
XLA Modules:
  0.0 52.5 jit_solution(1411648675853514269)
XLA Ops:
  0.6 48.6 %decode.1 = (bf16[128,512]{1,0:T(8,128)(2,1)}, bf16[4,32,1024]{2,1,0:T(8,128)(2,1)}) custom-call(s32[32]{0:T(128)} %lens_hbm.1, bf16[128,1280]{1,0:T(8,128)(2,1)} %bitcast.11, bf16[1280,2048]{1,0:T(8,128)(2,1)} %bitcast.10, bf16[4,32,1024]{2,1,0:T(8,128)(2,1)} %bitcast.12, bf16[32,4,128,256]{3,2,1,0:T(8,128)(2,1)} %bitcast.9, s32[1,1280]{1,0:T(1,128)} %updated_hbm.1, ...), custom_call_target="tpu_custom_call" | custom-call | tf_op jit(solution)/shard_map/decode/pallas_call | solution.py:499
  49.2 1.6 %copy.14 = bf16[1,4,32,512]{3,2,1,0:T(8,128)(2,1)} copy(bf16[1,4,32,512]{3,2,1,0:T(8,128)(2,1)} %bitcast.14) | data formatting | bytes 262144
  50.8 1.7 %copy.15 = bf16[1,4,32,1024]{3,2,1,0:T(8,128)(2,1)} copy(bf16[1,4,32,1024]{3,2,1,0:T(8,128)(2,1)} %bitcast.13) | data formatting | bytes 524288

commit v4 on v3

--- a/solution.py
+++ b/solution.py
@@ -230,7 +230,8 @@
         packed_ref.at[owner_rows(me)], delta_buf.at[my_rows], local_sem.at[1]
     )
     own_delta.start()
-    for g in range(heads):
+    early = (heads + 1) // 2
+    for g in range(early):
         query_copy(g).start()
 
     hidden_load.wait()
@@ -297,6 +298,8 @@
 
     for k in range(1, n_half):
         sum_copy(k).start()
+    for g in range(early, heads):
+        query_copy(g).start()
 
     def tail_copy(i, source, target):
         return pltpu.make_async_remote_copy(
@@ -357,6 +360,10 @@
             at = pl.ds(g * blocks + block, 1)
             back_stats[0, at, :] = jnp.sum(jnp.where(eye, m, 0.0), 0, keepdims=True)
             back_stats[1, at, :] = jnp.sum(jnp.where(eye, l, 0.0), 0, keepdims=True)
+        return carry
+
+    def other_group_back(g, carry):
+        other_group(g, carry)
         back_copy(g).start()
         return carry
 
@@ -374,7 +381,6 @@
     cos_ref[...] = jnp.cos(angles)
     sin_ref[...] = jnp.where(first, -sine, sine)
 
-    early = (heads + 1) // 2
     lax.fori_loop(0, early, other_group, 0)
 
     for k in range(1, n_half):
@@ -389,8 +395,10 @@
     pair_buf[...] = jnp.where(upper == 0, sums[1], sums[0]).astype(bf16)
     pair_copy = tail_copy(2, pair_buf, pair_got)
     pair_copy.start()
-
-    lax.fori_loop(early, heads, other_group, 0)
+    for g in range(early):
+        back_copy(g).start()
+
+    lax.fori_loop(early, heads, other_group_back, 0)
     stats_copy = tail_copy(0, back_stats, got_stats)
     stats_copy.start()
 

time: 52.6 us -> 55.1 us (1.048)
  the two profiles are of different devices: /device:TPU:10 before, /device:TPU:0 now
where the time goes in v4:
time: 55.1 us; the launch traced here: 54.9 us
  Pallas kernels  51.1 us (93%)
  local copies, waits for them, and re-layouts  3.24 us (6%)
  between operations  0.64 us (1%)
    pallas_call x1, Pallas kernels, shards(): pl.pallas_call(functools.partial(kernel, (n_tp, n_pp, n_dp, width // bloc...  51.1 us
    unnamed x2, local copies, waits for them, and re-layouts  3.24 us

profile of v4, /device:TPU:0, one launch (start us, length us, event | category | flops | bytes accessed | tf_op | source)
XLA Modules:
  0.0 54.9 jit_solution(7117887728557002874)
XLA Ops:
  0.6 51.1 %decode.1 = (bf16[128,512]{1,0:T(8,128)(2,1)}, bf16[4,32,1024]{2,1,0:T(8,128)(2,1)}) custom-call(s32[32]{0:T(128)} %lens_hbm.1, bf16[128,1280]{1,0:T(8,128)(2,1)} %bitcast.11, bf16[1280,2048]{1,0:T(8,128)(2,1)} %bitcast.10, bf16[4,32,1024]{2,1,0:T(8,128)(2,1)} %bitcast.12, bf16[32,4,128,256]{3,2,1,0:T(8,128)(2,1)} %bitcast.9, s32[1,1280]{1,0:T(1,128)} %updated_hbm.1, ...), custom_call_target="tpu_custom_call" | custom-call | tf_op jit(solution)/shard_map/decode/pallas_call | solution.py:507
  51.7 1.6 %copy.14 = bf16[1,4,32,512]{3,2,1,0:T(8,128)(2,1)} copy(bf16[1,4,32,512]{3,2,1,0:T(8,128)(2,1)} %bitcast.14) | data formatting | bytes 262144
  53.3 1.7 %copy.15 = bf16[1,4,32,1024]{3,2,1,0:T(8,128)(2,1)} copy(bf16[1,4,32,1024]{3,2,1,0:T(8,128)(2,1)} %bitcast.13) | data formatting | bytes 524288
